TPU v7x, 256 devices: a whole 4x4x8 slice. The times are simulated.
256 devices in a mesh: tmpl: 32 (over y, z_lo, core), img: 8 (over z_hi, x).
Axes of the slice: x: 4, y: 4, z: 8 (z_hi: 2, z_lo: 4; z = z_hi * 4 + z_lo), core: 2. Of those that a mesh axis runs over, the one named last changes fastest.
Arguments:
- images: bfloat16 [2048, 32768], P(('tmpl', 'img')), may hold values from -43 to 43
- ctf_ids: int32 [2048], P(('tmpl', 'img')), may hold values from 0 to 7
- cotangent: float32 [2048], P(('tmpl', 'img')), may hold values from -6 to 6
- templates: bfloat16 [2048, 32768], P('tmpl'), may hold values from -1 to 1
- template_orient: int32 [2048], P('tmpl'), may hold values from 0 to 511
- ctf_table: float32 [8, 32768], replicated, may hold values from 0.25 to 1
- log_prior: float32 [512], replicated, may hold values from -4 to 4
Outputs:
- template_grad: bfloat16 [2048, 32768], P('tmpl', 'img')
- loglik: float32 [2048], P(('tmpl', 'img'))
- prior_grad: float32 [512], replicated
All inputs are finite; a program needn't handle non-finite values.
Results may differ from a plain program's by a relative error of at most 0.015.
Values may be sent and summed in bfloat16 or wider, within the bound.
A program may use at most 128 MiB of HBM per device.

v0:
```python
import jax
import jax.numpy as jnp
from jax import lax
from jax.sharding import PartitionSpec as P

HIGH = lax.Precision.HIGHEST


def local(images, ctf_ids, cotangent, templates, template_orient, ctf_table, log_prior):
    classes = ctf_table.shape[0]
    orients = log_prior.shape[0]
    own_rows = images.shape[0]
    width = images.shape[1]
    senders = lax.axis_size("tmpl")
    ctf_sq = ctf_table * ctf_table
    ids_round = ctf_ids.astype(jnp.bfloat16)
    cot_round = cotangent.astype(jnp.bfloat16)
    class_range = jnp.arange(classes, dtype=jnp.float32)
    gathered, ids_all, cot_all = (
        lax.all_gather(images, "tmpl", axis=0, tiled=True),
        lax.all_gather(ids_round, "tmpl", axis=0, tiled=True),
        lax.all_gather(cot_round, "tmpl", axis=0, tiled=True),
    )
    class_hot = (ids_all.astype(jnp.float32)[:, None] == class_range[None, :]).astype(jnp.float32)

    def weigh_block(pieces):
        rows, hot = pieces
        return (jnp.dot(hot, ctf_table, precision=HIGH) * rows.astype(jnp.float32)).astype(
            jnp.bfloat16
        )

    weighted = lax.map(
        weigh_block,
        (gathered.reshape(senders, own_rows, width), class_hot.reshape(senders, own_rows, classes)),
    )
    weighted = weighted.reshape(senders * own_rows, width)
    tmpl_wide = templates.astype(jnp.float32)
    norms = jnp.dot(ctf_sq, (tmpl_wide * tmpl_wide).T, precision=HIGH)
    orient_hot = (template_orient[:, None] == jnp.arange(orients, dtype=jnp.int32)[None, :]).astype(
        jnp.float32
    )
    prior_terms = jnp.dot(orient_hot, log_prior, precision=HIGH)
    scores = jnp.einsum("if,jf->ij", weighted, templates, preferred_element_type=jnp.float32)
    scores = scores - 0.5 * jnp.dot(class_hot, norms, precision=HIGH) + prior_terms[None, :]
    local_top = jnp.max(scores, axis=1)
    top = lax.pmax(local_top, "tmpl")
    total = lax.psum(jnp.sum(jnp.exp(scores - top[:, None]), axis=1), "tmpl")
    loglik_all = top + jnp.log(total)
    probs = cot_all.astype(jnp.float32)[:, None] * jnp.exp(scores - loglik_all[:, None])
    probs_b = probs.astype(jnp.bfloat16)
    prior_local = jnp.dot(jnp.sum(probs, axis=0), orient_hot, precision=HIGH)
    prior_grad = lax.psum(prior_local, ("tmpl", "img"))
    direct = jnp.einsum("ij,if->jf", probs_b, weighted, preferred_element_type=jnp.float32)
    class_weight = jnp.dot(probs_b.astype(jnp.float32).T, class_hot, precision=HIGH)
    partial_value = direct - tmpl_wide * jnp.dot(class_weight, ctf_sq, precision=HIGH)
    template_grad = lax.psum_scatter(
        partial_value.astype(jnp.bfloat16), "img", scatter_dimension=1, tiled=True
    )
    loglik = lax.dynamic_slice_in_dim(loglik_all, lax.axis_index("tmpl") * own_rows, own_rows)
    return (template_grad, loglik, prior_grad)


def solution(mesh):
    placed = (
        P(("tmpl", "img"), None),
        P(("tmpl", "img")),
        P(("tmpl", "img")),
        P("tmpl", None),
        P("tmpl"),
        P(),
        P(),
    )
    return jax.shard_map(
        local,
        mesh=mesh,
        in_specs=placed,
        out_specs=(P("tmpl", "img"), P(("tmpl", "img")), P()),
        check_vma=False,
    )
```

profile of v0, /device:TPU:1, one launch (start us, length us, event | category | flops | bytes accessed | tf_op | source)
XLA Modules:
  0.0 519.1 jit_solution(3799834816062491419)
XLA Ops:
  11.7 71.4 %all-reduce.2 = (bf16[256]{0:T(256)(128)(2,1)S(1)}, bf16[256]{0:T(256)(128)(2,1)S(1)}) all-reduce(bf16[256]{0:T(256)(128)(2,1)S(1)} %dynamic-update-slice.1, bf16[256]{0:T(256)(128)(2,1)S(1)} %dynamic-update-slice), channel_id=1, replica_groups=mesh['tmpl'=32,'img'=8] {'tmpl'}, use_global_device_ids=true, to_apply=%add.1 | all-reduce | flops 512 | bytes 2048
  84.2 8.5 %fusion.10 = f32[8,64]{1,0:T(8,128)S(1)} fusion(bf16[64,32768]{1,0:T(8,128)(2,1)} %param.12, f32[8,32768]{1,0:T(8,128)} %param.14), kind=kOutput, calls=%fused_computation.14 | convolution fusion | flops 205783040 | bytes 5244928 | tf_op jit(solution)/shard_map/dot_general | solution.py:38
  92.7 22.2 %all-gather.2.cloned.1.call-done = bf16[256,32768]{1,0:T(8,128)(2,1)} async-done(((bf16[8,32768]{1,0:T(8,128)(2,1)}), bf16[256,32768]{1,0:T(8,128)(2,1)}) %all-gather.2.cloned.1.call-update) | async-done | bytes 16777232 | tf_op jit(solution)/shard_map/all_gather | solution.py:20
  115.0 101.1 %while.10 = (s32[]{:T(128)}, bf16[32,8,32768]{2,1,0:T(8,128)(2,1)}, f32[32,8,8]{2,1,0:T(8,128)S(1)}, f32[8,32768]{1,0:T(8,128)}, bf16[32,8,32768]{2,1,0:T(8,128)(2,1)}, /*index=5*/s32[]{:T(128)}) while((s32[]{:T(128)}, bf16[32,8,32768]{2,1,0:T(8,128)(2,1)}, f32[32,8,8]{2,1,0:T(8,128)S(1)}, f32[8,32768]{1,0:T(8,128)}, ...), condition=%wide.region_1.2_spmd, body=%wide.region_0.1_spmd.sunk | while | flops 25952256 | bytes 2102341 | solution.py:32
  121.3 3.2 fusion.38
  124.4 3.2 fusion.38
  130.8 3.2 fusion.38
  137.1 3.2 fusion.38
  143.4 3.2 fusion.38
  149.7 3.2 fusion.38
  156.0 3.2 fusion.38
  165.5 3.2 fusion.38
  168.7 3.2 fusion.38
  178.2 3.2 fusion.38
  181.4 3.2 fusion.38
  190.8 3.2 fusion.38
  194.0 3.2 fusion.38
  216.1 12.2 %fusion.8 = f32[256,64]{0,1:T(8,128)S(1)} fusion(bf16[64,32768]{1,0:T(8,128)(2,1)} %param.12, bf16[32,8,32768]{2,1,0:T(8,128)(2,1)} %get-tuple-element.30), kind=kOutput, calls=%fused_computation.11 | convolution fusion | flops 1073741824 | bytes 21037056 | tf_op jit(solution)/shard_map/if,jf->ij/dot_general | solution.py:43
  228.7 67.0 %pmax.7 = f32[256]{0:T(256)S(1)} all-reduce(f32[256]{0:T(256)S(1)} %get-tuple-element.43), channel_id=1, replica_groups=mesh['tmpl'=32,'img'=8] {'tmpl'}, use_global_device_ids=true, to_apply=%region_3.4 | all-reduce | flops 256 | bytes 2048 | tf_op jit(solution)/shard_map/pmax | solution.py:46
  295.7 72.1 %psum.14 = f32[256]{0:T(256)S(1)} all-reduce(f32[256]{0:T(256)S(1)} %exponential_reduce_fusion), channel_id=1, replica_groups=mesh['tmpl'=32,'img'=8] {'tmpl'}, use_global_device_ids=true, to_apply=%region_5.6 | all-reduce | flops 256 | bytes 2048 | tf_op jit(solution)/shard_map/psum | solution.py:47
  368.0 8.7 %convolution_multiply_fusion.1 = f32[64,32768]{1,0:T(8,128)S(1)} fusion(f32[64,8]{1,0:T(8,128)S(1)} %fusion.16, bf16[64,32768]{1,0:T(8,128)(2,1)} %param.12, f32[8,32768]{1,0:T(8,128)S(1)} %copy-done.1), kind=kOutput, calls=%fused_computation.7 | convolution fusion | flops 205783040 | bytes 13633536 | tf_op jit(solution)/shard_map/dot_general | solution.py:55
  376.7 11.0 %fusion.6 = bf16[64,32768]{1,0:T(8,128)(2,1)} fusion(f32[64,32768]{1,0:T(8,128)S(1)} %convolution_multiply_fusion.1, bf16[32,8,32768]{2,1,0:T(8,128)(2,1)} %get-tuple-element.30, f32[256,64]{0,1:T(8,128)S(1)} %get-tuple-element.44, f32[256]{0:T(256)S(1)} %log_add_fusion, f32[256]{0:T(256)S(1)} %convert_element_type.37), kind=kOutput, calls=%fused_computation.9 | convolution fusion | flops 1077985280 | bytes 29427712 | tf_op jit(solution)/shard_map/ij,if->jf/dot_general | solution.py:53
  388.7 97.7 %psum.15 = f32[512]{0:T(512)} all-reduce(f32[512]{0:T(512)S(1)} %bitcast.39), channel_id=1, replica_groups=mesh['tmpl'=32,'img'=8] {'tmpl','img'}, use_global_device_ids=true, to_apply=%region_8.9 | all-reduce | flops 512 | bytes 4096 | tf_op jit(solution)/shard_map/psum | solution.py:52
  486.4 25.9 %reduce-scatter.2.cloned.1.call-done = bf16[64,4096]{1,0:T(8,128)(2,1)} async-done(((bf16[64,32768]{1,0:T(8,128)(2,1)}), bf16[64,4096]{1,0:T(8,128)(2,1)}) %reduce-scatter.2.cloned.1.call-update) | async-done | bytes 524304 | tf_op jit(solution)/shard_map/reduce_scatter | solution.py:56
  (49 shorter events, 66.2 us)
Async XLA Ops:
  7.2 76.1 %copy-start = (f32[512]{0:T(512)S(1)}, f32[512]{0:T(512)}, u32[]{:S(2)}) copy-start(f32[512]{0:T(512)} %param.15) | copy-start | bytes 6148
  7.2 107.8 %all-gather.2.cloned.1.call-start = ((), (), s32[]{:S(2)}) async-start(), calls=%async_computation.1 | async-start | bytes 17301504 | tf_op jit(solution)/shard_map/all_gather | solution.py:20
  7.9 504.4 %reduce-scatter.2.cloned.1.call-start = ((), (), s32[]{:S(2)}) async-start(), calls=%async_computation.2 | async-start | bytes 4718592 | tf_op jit(solution)/shard_map/reduce_scatter | solution.py:56
  216.1 151.9 %copy-start.1 = (f32[8,32768]{1,0:T(8,128)S(1)}, f32[8,32768]{1,0:T(8,128)}, u32[]{:S(2)}) copy-start(f32[8,32768]{1,0:T(8,128)} %get-tuple-element.96) | copy-start | bytes 3145732
  376.7 11.8 %copy-start.2 = (s32[64]{0:T(128)S(1)}, s32[64]{0:T(128)}, u32[]{:S(2)}) copy-start(s32[64]{0:T(128)} %param.13) | copy-start | bytes 772
Sparse Core Ops, SparseCore 0:
  9.9 105.0 all-gather.1
  387.8 124.3 reduce-scatter.1
where the time goes:
time: 521 us; the launch traced here: 519 us
  blocking collectives  308 us (59%)
  matrix products  143 us (27%)
  waiting for transfers between devices  48.8 us (9%)
  between operations  14.8 us (3%)
    dot_general x32, matrix products, weigh_block(): jnp.dot(hot, ctf_table, precision=HIGH) * rows.astype(jnp.float32)  101 us
    psum x1, blocking collectives, local(): prior_grad = lax.psum(prior_local, ('tmpl', 'img'))  97.7 us
    psum x1, blocking collectives, local(): total = lax.psum(jnp.sum(jnp.exp(scores - top[:, None]), axis=1), 'tmpl')  72.1 us
    unnamed x1, blocking collectives  71.4 us
    pmax x1, blocking collectives, local(): top = lax.pmax(local_top, 'tmpl')  67 us
    reduce_scatter x1, waiting for transfers between devices, local(): lax.psum_scatter(partial_value.astype(jnp.bfloat16), 'img', scatter_dimen...  25.9 us
    all_gather x1, waiting for transfers between devices, local(): lax.all_gather(images, 'tmpl', axis=0, tiled=True)  22.2 us
    dot_general x1, matrix products, local(): jnp.einsum('if,jf->ij', weighted, templates, preferred_element_type=jnp.f...  12.2 us
  transfers between devices with their start and end apart: 2, of which 2 were waited for; matrix products, arithmetic and copies ran while one was open for 3% of the time, Pallas kernels for 0%

commit v1 on v0

v1 whole, which is shorter than its diff:
```python
import jax
import jax.numpy as jnp
from jax import lax
from jax.sharding import PartitionSpec as P

HIGH = lax.Precision.HIGHEST


def local(images, ctf_ids, cotangent, templates, template_orient, ctf_table, log_prior):
    classes = ctf_table.shape[0]
    orients = log_prior.shape[0]
    own_rows = images.shape[0]
    ctf_sq = ctf_table * ctf_table
    class_range = jnp.arange(classes, dtype=jnp.int32)
    own_hot = (ctf_ids[:, None] == class_range[None, :]).astype(jnp.float32)
    own_ctf = jnp.dot(own_hot, ctf_table, precision=HIGH)
    weighted = (own_ctf * images.astype(jnp.float32)).astype(jnp.bfloat16)
    cot_round = cotangent.astype(jnp.bfloat16).astype(jnp.float32)
    small = jnp.stack([ctf_ids.astype(jnp.float32), cot_round], axis=1)
    small = lax.all_gather(small, "tmpl", axis=0, tiled=True)
    weighted = lax.all_gather(weighted, "tmpl", axis=0, tiled=True)
    class_hot = (small[:, :1] == class_range[None, :].astype(jnp.float32)).astype(jnp.float32)
    cot_all = small[:, 1]
    tmpl_wide = templates.astype(jnp.float32)
    norms = jnp.dot(ctf_sq, (tmpl_wide * tmpl_wide).T, precision=HIGH)
    orient_hot = (template_orient[:, None] == jnp.arange(orients, dtype=jnp.int32)[None, :]).astype(
        jnp.float32
    )
    prior_terms = jnp.dot(orient_hot, log_prior, precision=HIGH)
    scores = jnp.einsum("if,jf->ij", weighted, templates, preferred_element_type=jnp.float32)
    scores = scores - 0.5 * jnp.dot(class_hot, norms, precision=HIGH) + prior_terms[None, :]
    local_top = jnp.max(scores, axis=1)
    local_sum = jnp.sum(jnp.exp(scores - local_top[:, None]), axis=1)
    stats = lax.all_gather(jnp.stack([local_top, local_sum]), "tmpl", axis=0)
    top = jnp.max(stats[:, 0], axis=0)
    total = jnp.sum(stats[:, 1] * jnp.exp(stats[:, 0] - top[None, :]), axis=0)
    loglik_all = top + jnp.log(total)
    probs = cot_all[:, None] * jnp.exp(scores - loglik_all[:, None])
    probs_b = probs.astype(jnp.bfloat16)
    prior_local = jnp.dot(jnp.sum(probs, axis=0), orient_hot, precision=HIGH)
    prior_grad = lax.psum(prior_local, ("tmpl", "img"))
    direct = jnp.einsum("ij,if->jf", probs_b, weighted, preferred_element_type=jnp.float32)
    class_weight = jnp.dot(probs_b.astype(jnp.float32).T, class_hot, precision=HIGH)
    partial_value = direct - tmpl_wide * jnp.dot(class_weight, ctf_sq, precision=HIGH)
    template_grad = lax.psum_scatter(
        partial_value.astype(jnp.bfloat16), "img", scatter_dimension=1, tiled=True
    )
    loglik = lax.dynamic_slice_in_dim(loglik_all, lax.axis_index("tmpl") * own_rows, own_rows)
    return (template_grad, loglik, prior_grad)


def solution(mesh):
    placed = (
        P(("tmpl", "img"), None),
        P(("tmpl", "img")),
        P(("tmpl", "img")),
        P("tmpl", None),
        P("tmpl"),
        P(),
        P(),
    )
    return jax.shard_map(
        local,
        mesh=mesh,
        in_specs=placed,
        out_specs=(P("tmpl", "img"), P(("tmpl", "img")), P()),
        check_vma=False,
    )
```

time: 521 us -> 320 us (0.61)
  blocking collectives: 308 us -> 188 us
  matrix products: 143 us -> 42.6 us
  waiting for transfers between devices: 48.8 us -> 72.3 us
    dot_general x32 -> x1, matrix products: 101 us -> 2.83 us  [local(): own_ctf = jnp.dot(own_hot, ctf_table, precision=HIGH)]
    all_gather x0 -> x2, blocking collectives: none -> 88.9 us  [the longest x1 46.1 us: local(): small = lax.all_gather(small, 'tmpl', axis=0, tiled=True)]
    psum x1 -> x0, blocking collectives: 72.1 us -> none  [local(): total = lax.psum(jnp.sum(jnp.exp(scores - top[:, None]), axis=1), 'tmpl')]
    unnamed x1 -> x0, blocking collectives: 71.4 us -> none
    pmax x1 -> x0, blocking collectives: 67 us -> none  [local(): top = lax.pmax(local_top, 'tmpl')]
    all_gather x1, waiting for transfers between devices: 22.2 us -> 47.6 us  [local(): weighted = lax.all_gather(weighted, 'tmpl', axis=0, tiled=True)]
  transfers between devices with their start and end apart: 2 -> 2, of which waited for: 2 -> 2; matrix products, arithmetic and copies ran while one was open for 3% -> 4% of each run, Pallas kernels for 0% -> 0%
where the time goes in v1:
time: 320 us; the launch traced here: 319 us
  blocking collectives  188 us (59%)
  waiting for transfers between devices  72.3 us (23%)
  matrix products  42.6 us (13%)
  between operations  14.1 us (4%)
    psum x1, blocking collectives, local(): prior_grad = lax.psum(prior_local, ('tmpl', 'img'))  98.9 us
    all_gather x1, waiting for transfers between devices, local(): weighted = lax.all_gather(weighted, 'tmpl', axis=0, tiled=True)  47.6 us
    all_gather x1, blocking collectives, local(): small = lax.all_gather(small, 'tmpl', axis=0, tiled=True)  46.1 us
    all_gather x1, blocking collectives, local(): stats = lax.all_gather(jnp.stack([local_top, local_sum]), 'tmpl', axis=0)  42.8 us
    reduce_scatter x1, waiting for transfers between devices, local(): lax.psum_scatter(partial_value.astype(jnp.bfloat16), 'img', scatter_dimen...  24.7 us
    dot_general x1, matrix products, local(): jnp.einsum('if,jf->ij', weighted, templates, preferred_element_type=jnp.f...  12.3 us
    dot_general x1, matrix products, local(): jnp.dot(class_weight, ctf_sq, precision=HIGH)  11 us
    dot_general x1, matrix products, local(): norms = jnp.dot(ctf_sq, (tmpl_wide * tmpl_wide).T, precision=HIGH)  8.54 us
  transfers between devices with their start and end apart: 2, of which 2 were waited for; matrix products, arithmetic and copies ran while one was open for 4% of the time, Pallas kernels for 0%

profile of v1, /device:TPU:1, one launch (start us, length us, event | category | flops | bytes accessed | tf_op | source)
XLA Modules:
  0.0 319.2 jit_solution(13813910402338306869)
XLA Ops:
  7.2 0.0 all-gather.5.cloned.1.call-start
  7.2 2.8 fusion.2
  10.1 0.0 all-gather.5.cloned.1.call-update
  10.1 0.0 reduce-scatter.2.cloned.1.call-start
  10.1 0.7 convert_bitcast_fusion
  10.8 0.7 bitcast_convert_fusion
  11.5 46.1 %all-gather.1 = f32[32,8,2]{1,2,0:T(2,128)S(1)} all-gather(f32[1,8,2]{1,2,0:T(2,128)S(1)} %maximum_bitcast_fusion.1), channel_id=1, replica_groups=mesh['tmpl'=32,'img'=8] {'tmpl'}, dimensions={0}, use_global_device_ids=true | all-gather | bytes 2112 | tf_op jit(solution)/shard_map/all_gather | solution.py:20
  57.6 0.1 reshape.25
  57.7 0.8 convolution_bitcast_fusion
  58.5 8.5 %fusion.3 = f32[8,64]{1,0:T(8,128)S(1)} fusion(bf16[64,32768]{1,0:T(8,128)(2,1)} %param.10, f32[8,32768]{1,0:T(8,128)} %param.12), kind=kOutput, calls=%fused_computation.6 | convolution fusion | flops 205783040 | bytes 5244928 | tf_op jit(solution)/shard_map/dot_general | solution.py:25
  67.1 47.6 %all-gather.5.cloned.1.call-done = bf16[256,32768]{1,0:T(8,128)(2,1)} async-done(((bf16[8,32768]{1,0:T(8,128)(2,1)}), bf16[256,32768]{1,0:T(8,128)(2,1)}) %all-gather.5.cloned.1.call-update) | async-done | bytes 16777232 | tf_op jit(solution)/shard_map/all_gather | solution.py:21
  114.6 12.3 %fusion.31 = f32[256,64]{0,1:T(8,128)S(1)} fusion(bf16[256,32768]{1,0:T(8,128)(2,1)} %all-gather.5.cloned.1.call-done, bf16[64,32768]{1,0:T(8,128)(2,1)} %param.10), kind=kOutput, calls=%fused_computation.47 | convolution fusion | flops 1073741824 | bytes 21037056 | tf_op jit(solution)/shard_map/if,jf->ij/dot_general | solution.py:30
  126.9 0.3 fusion.30
  127.3 42.8 %all-gather.2 = f32[32,2,256]{2,1,0:T(2,128)S(1)} all-gather(f32[1,2,256]{2,1,0:T(2,128)S(1)} %maximum_bitcast_fusion), channel_id=2, replica_groups=mesh['tmpl'=32,'img'=8] {'tmpl'}, dimensions={0}, use_global_device_ids=true | all-gather | bytes 67584 | tf_op jit(solution)/shard_map/all_gather | solution.py:34
  170.1 0.1 fusion.28
  170.2 0.3 fusion.8
  170.5 6.3 %fusion.24 = f32[64,32768]{1,0:T(8,128)} fusion(bf16[256,32768]{1,0:T(8,128)(2,1)S(1)} %copy-done.1, f32[256,64]{0,1:T(8,128)S(1)} %get-tuple-element.9, f32[256]{0:T(256)S(1)} %log_add_fusion, f32[256]{0:T(256)S(1)} %bitcast.43), kind=kOutput, calls=%fused_computation.34 | convolution fusion | flops 1073790976 | bytes 25233408 | tf_op jit(solution)/shard_map/ij,if->jf/dot_general | solution.py:42
  176.7 11.0 %fusion.1 = bf16[64,32768]{1,0:T(8,128)(2,1)} fusion(f32[64,32768]{1,0:T(8,128)} %fusion.24, f32[64,8]{0,1:T(8,128)S(1)} %fusion.8, bf16[64,32768]{1,0:T(8,128)(2,1)S(1)} %copy-done.2, f32[8,32768]{1,0:T(8,128)S(1)} %copy-done.3), kind=kOutput, calls=%fused_computation.2 | convolution fusion | flops 209977344 | bytes 17827840 | tf_op jit(solution)/shard_map/dot_general | solution.py:44
  187.8 0.0 reduce-scatter.2.cloned.1.call-update
  187.8 0.6 dynamic_slice.3
  188.4 0.1 fusion.18
  188.5 0.2 fusion.11
  188.8 98.9 %psum.7 = f32[512]{0:T(512)} all-reduce(f32[512]{0:T(512)S(1)} %bitcast.49), channel_id=1, replica_groups=mesh['tmpl'=32,'img'=8] {'tmpl','img'}, use_global_device_ids=true, to_apply=%region_6.0 | all-reduce | flops 512 | bytes 4096 | tf_op jit(solution)/shard_map/psum | solution.py:41
  287.6 24.7 %reduce-scatter.2.cloned.1.call-done = bf16[64,4096]{1,0:T(8,128)(2,1)} async-done(((bf16[64,32768]{1,0:T(8,128)(2,1)}), bf16[64,4096]{1,0:T(8,128)(2,1)}) %reduce-scatter.2.cloned.1.call-update) | async-done | bytes 524304 | tf_op jit(solution)/shard_map/reduce_scatter | solution.py:45
  (18 shorter events, 0.1 us)
Async XLA Ops:
  7.2 50.5 %copy-start = (f32[512]{0:T(512)S(1)}, f32[512]{0:T(512)}, u32[]{:S(2)}) copy-start(f32[512]{0:T(512)} %param.13) | copy-start | bytes 6148
  7.2 107.5 %all-gather.5.cloned.1.call-start = ((), (), s32[]{:S(2)}) async-start(), calls=%async_computation.1 | async-start | bytes 17301504 | tf_op jit(solution)/shard_map/all_gather | solution.py:21
  10.1 302.2 %reduce-scatter.2.cloned.1.call-start = ((), (), s32[]{:S(2)}) async-start(), calls=%async_computation.2 | async-start | bytes 4718592 | tf_op jit(solution)/shard_map/reduce_scatter | solution.py:45
  114.6 55.8 %copy-start.1 = (bf16[256,32768]{1,0:T(8,128)(2,1)S(1)}, bf16[256,32768]{1,0:T(8,128)(2,1)}, u32[]{:S(2)}) copy-start(bf16[256,32768]{1,0:T(8,128)(2,1)} %all-gather.5.cloned.1.call-done) | copy-start | bytes 50331652
  170.5 6.3 %copy-start.2 = (bf16[64,32768]{1,0:T(8,128)(2,1)S(1)}, bf16[64,32768]{1,0:T(8,128)(2,1)}, u32[]{:S(2)}) copy-start(bf16[64,32768]{1,0:T(8,128)(2,1)} %param.10) | copy-start | bytes 12582916
  170.5 6.3 %copy-start.3 = (f32[8,32768]{1,0:T(8,128)S(1)}, f32[8,32768]{1,0:T(8,128)}, u32[]{:S(2)}) copy-start(f32[8,32768]{1,0:T(8,128)} %param.12) | copy-start | bytes 3145732
  176.7 11.8 %copy-start.4 = (s32[64]{0:T(128)S(1)}, s32[64]{0:T(128)}, u32[]{:S(2)}) copy-start(s32[64]{0:T(128)} %param.11) | copy-start | bytes 772
Sparse Core Ops, SparseCore 0:
  10.4 104.1 all-gather.4
  187.9 124.3 reduce-scatter.1

commit v2 on v1

v2 whole, which is shorter than its diff:
```python
import functools

import jax
import jax.numpy as jnp
from jax import lax
from jax.experimental import pallas as pl
from jax.experimental.pallas import tpu as pltpu
from jax.sharding import PartitionSpec as P

HIGH = lax.Precision.HIGHEST
MESH = pl.DeviceIdType.MESH
F32, BF16 = jnp.float32, jnp.bfloat16

Y, ZL, CORES, ZH, X = 4, 4, 2, 2, 4
A = 2
B = ZL // A
ZZ = ZH * A
K = A * CORES
PIECES = Y * B
FGROUP = ZZ * X * CORES

ORDER = (
    [(db, 0) for db in range(B)]
    + [(db, dy) for db in range(B) for dy in (1, 3)]
    + [(db, 2) for db in range(B)]
)
PIECE = {step: index for index, step in enumerate(ORDER)}
GROUPS = ((0, 3 * B), (3 * B, B))


def nt_dot(a, b, precision=None):
    return lax.dot_general(
        a, b, (((1,), (1,)), ((), ())), precision=precision, preferred_element_type=F32
    )


def tn_dot(a, b, precision=None):
    return lax.dot_general(
        a, b, (((0,), (0,)), ((), ())), precision=precision, preferred_element_type=F32
    )


def kernel(
    wsrc, templates, ctf, meta, tmeta, grad, loglik, prior,
    w, s, r1, r2, r3, t2, ctf_own, metas, tmetas, nz, nx, nc, cz, cx, cc, stats, bins,
    pall, p2, gout, sems,
):
    t, g = lax.axis_index("tmpl"), lax.axis_index("img")
    core, zl, y = t % CORES, (t // CORES) % ZL, t // (CORES * ZL)
    x, zh = g % X, g // X
    a, b = zl // B, zl % B
    zz = zh * A + a
    k = a * CORES + core
    rows, half = w.shape[-2], w.shape[-1]
    block = rows // 2
    cols = 2 * half
    depth, orient_rows = s.shape[-1], 4
    own_t = templates.shape[0]
    owned = PIECES * block

    def device(dy=0, db=0, dz=0, dx=0, dc=0):
        y2, b2, z2, x2, c2 = (y + dy) % Y, (b + db) % B, (zz + dz) % ZZ, (x + dx) % X, (core + dc) % CORES
        zl2 = (z2 % A) * B + b2
        return ((y2 * ZL + zl2) * CORES + c2, (z2 // A) * X + x2)

    def device_k(da, dc):
        a2, c2 = (a + da) % A, (core + dc) % CORES
        return ((y * ZL + a2 * B + b) * CORES + c2, g), a2 * CORES + c2

    used = [0]
    sent = []

    def take():
        used[0] += 1
        return sems.at[used[0] - 1]

    def remote(src, dst, dev):
        copy = pltpu.make_async_remote_copy(
            src_ref=src, dst_ref=dst, send_sem=take(), recv_sem=take(),
            device_id=dev, device_id_type=MESH,
        )
        copy.start()
        sent.append(copy)
        return copy

    def here(src, dst):
        copy = pltpu.make_async_copy(src, dst, take())
        copy.start()
        return copy

    ring_f = [(dz, dx, dc) for dz in range(ZZ) for dx in range(X) for dc in range(CORES)][1:]
    ring_p = ORDER[1:]
    ring_k = [(da, dc) for da in range(A) for dc in range(CORES)][1:]

    mine = pl.ds(pl.multiple_of((g * K + k) * cols, 128), cols)
    load_ctf = here(ctf.at[:, mine], ctf_own)
    load_t = [
        here(
            templates.at[:, pl.ds(pl.multiple_of((g * K + k) * cols + q * half, 128), half)],
            t2.at[q, k],
        )
        for q in range(2)
    ]
    barrier = pltpu.get_barrier_semaphore()
    for dz, dx, dc in ring_f:
        pl.semaphore_signal(barrier, inc=1, device_id=device(dz=dz, dx=dx, dc=dc), device_id_type=MESH)
    for db, dy in ring_p:
        pl.semaphore_signal(barrier, inc=1, device_id=device(dy=dy, db=db), device_id_type=MESH)
    pl.semaphore_wait(barrier, len(ring_f) + len(ring_p))

    exchange = {}
    z_order = sorted(range(ZZ), key=lambda dz: min(dz, ZZ - dz))
    own_copy = here(wsrc.at[g * K + k], w.at[0, 0, 0, 0])
    for dz in z_order:
        for dx in range(X):
            for dc in range(CORES):
                if (dz, dx, dc) == (0, 0, 0):
                    continue
                z2, x2, c2 = (zz + dz) % ZZ, (x + dx) % X, (core + dc) % CORES
                dest = ((z2 // A) * X + x2) * K + (z2 % A) * CORES + c2
                back = ((-dz) % ZZ, (-dc) % CORES, (-dx) % X)
                exchange.setdefault(back[0], []).append(
                    remote(wsrc.at[dest], w.at[0, back[0], back[1], back[2]], device(dz=dz, dx=dx, dc=dc))
                )
    exchange_t, exchange_tm = [], []
    for da, dc in ring_k:
        dev, k2 = device_k(da, dc)
        for q in range(2):
            start = pl.multiple_of((g * K + k2) * cols + q * half, 128)
            exchange_t.append(remote(templates.at[:, pl.ds(start, half)], t2.at[q, k], dev))
        exchange_tm.append(remote(tmeta, tmetas.at[k], dev))
    exchange_m = [
        remote(meta, metas.at[PIECE[((-db) % B, (-dy) % Y)]], device(dy=dy, db=db)) for db, dy in ring_p
    ]

    from_b, from_y = {}, {}

    def send_y(db, dz):
        piece = PIECE[(db, 0)]
        for step in (1, 3):
            from_y[(db, (-step) % Y, dz)] = remote(
                w.at[piece, dz], w.at[PIECE[(db, (-step) % Y)], dz], device(dy=step)
            )

    own_copy.wait()
    for dz in z_order:
        for copy in exchange[dz]:
            copy.wait_recv()
        for db in range(1, B):
            from_b[((-db) % B, dz)] = remote(
                w.at[0, dz], w.at[PIECE[((-db) % B, 0)], dz], device(db=db)
            )
        send_y(0, dz)

    load_ctf.wait()
    for copy in load_t:
        copy.wait()
    for copy in exchange_t + exchange_tm + exchange_m:
        copy.wait_recv()
    metas[0] = meta[...]
    tmetas[k] = tmeta[...]
    square = ctf_own[...] * ctf_own[...]
    norm_part = jnp.zeros((square.shape[0], depth), F32)
    for q in range(2):
        wide = t2[q].reshape(depth, half).astype(F32)
        norm_part += nt_dot(square[:, q * half : (q + 1) * half], wide * wide, HIGH)

    def sum_over(buffer, me, size, value, name):
        buffer[me] = value
        return [
            remote(buffer.at[me], buffer.at[me], device(**{name: step})) for step in range(1, size)
        ]

    def total_of(buffer, copies):
        for copy in copies:
            copy.wait_recv()
        total = buffer[0]
        for index in range(1, buffer.shape[0]):
            total = total + buffer[index]
        return total

    norm_copies = sum_over(nz, zz, ZZ, norm_part, "dz")

    def score(piece):
        lhs = w[piece].reshape(FGROUP * rows, half)
        out = nt_dot(lhs, t2[...].reshape(2 * depth, half))
        out = out.reshape(ZZ, CORES, X, 2, block, 2 * depth)
        value = out[:, :, :, 0, :, :depth] + out[:, :, :, 1, :, depth:]
        for dz in range(ZZ):
            for dc in range(CORES):
                for dx in range(X):
                    s[dc, dx, dz, piece] = value[dz, dc, dx]

    for db in range(1, B):
        for dz in z_order:
            from_b[(db, dz)].wait_recv()
            send_y(db, dz)
    norm_copies = sum_over(nx, x, X, total_of(nz, norm_copies), "dx")
    for db in range(B):
        score(PIECE[(db, 0)])

    far = {}
    for db in range(B):
        for dz in z_order:
            for side, step in ((0, 1), (1, 3)):
                source = (-step) % Y
                from_y[(db, source, dz)].wait_recv()
                far[(db, dz, side)] = remote(
                    w.at[PIECE[(db, source)], dz, side], w.at[PIECE[(db, 2)], dz, side], device(dy=step)
                )
    norm_copies = sum_over(nc, core, CORES, total_of(nx, norm_copies), "dc")

    def reduce_core(first, count):
        span = pl.ds(first, count)
        return remote(s.at[1, :, :, span], r1.at[:, :, span], device(dc=1))

    def reduce_x(first, count, copy):
        span = pl.ds(first, count)
        copy.wait_recv()
        s[0, :, :, span] = s[0, :, :, span] + r1[:, :, span]
        return [
            remote(s.at[0, dx, :, span], r2.at[dx - 1, :, span], device(dx=dx)) for dx in range(1, X)
        ]

    def reduce_z(first, count, copies):
        span = pl.ds(first, count)
        for copy in copies:
            copy.wait_recv()
        total = s[0, 0, :, span]
        for index in range(X - 1):
            total = total + r2[index, :, span]
        s[0, 0, :, span] = total
        return [
            remote(s.at[0, 0, dz, span], r3.at[dz - 1, span], device(dz=dz)) for dz in range(1, ZZ)
        ]

    for db in range(B):
        for dy in (1, 3):
            score(PIECE[(db, dy)])
    copies = reduce_core(*GROUPS[0])
    norms = total_of(nc, norm_copies)
    copies = reduce_x(*GROUPS[0], copies)
    for db in range(B):
        for dz in z_order:
            for side in range(2):
                far[(db, dz, side)].wait_recv()
        score(PIECE[(db, 2)])
    later = reduce_core(*GROUPS[1])
    copies = reduce_z(*GROUPS[0], copies)
    later = reduce_x(*GROUPS[1], later)
    later = reduce_z(*GROUPS[1], later)
    for copy in copies + later:
        copy.wait_recv()
    scores = s[0, 0, 0]
    for index in range(ZZ - 1):
        scores = scores + r3[index]
    scores = scores.reshape(owned, depth)

    info = metas[...].reshape(owned, 128)
    ids, cot = info[:, 0:1], info[:, 64:65]
    lane8 = lax.broadcasted_iota(jnp.int32, (1, 128), 1)
    prior_row = jnp.concatenate(
        [jnp.where(lane8 < 64, tmetas[i, 0:1, :], tmetas[i + 1, 0:1, :]) for i in range(0, K, 2)], axis=1
    )
    orient_row = jnp.concatenate(
        [jnp.where(lane8 < 64, tmetas[i, 1:2, :], tmetas[i + 1, 1:2, :]) for i in range(0, K, 2)], axis=1
    )
    norm_rows = jnp.zeros((owned, depth), F32)
    for c in range(norms.shape[0]):
        norm_rows = jnp.where(ids == float(c), norms[c : c + 1, :], norm_rows)
    scores = scores - 0.5 * norm_rows + prior_row
    top = jnp.max(scores, axis=1, keepdims=True)
    total = jnp.sum(jnp.exp(scores - top), axis=1, keepdims=True)
    sub = lax.broadcasted_iota(jnp.int32, (owned, 128), 0)
    lane = lax.broadcasted_iota(jnp.int32, (owned, 128), 1)
    target = sub % block
    for index, (db, dy) in enumerate(ORDER):
        place = ((y + dy) % Y) * B + (b + db) % B
        target = target + jnp.where(sub // block == index, place * block, 0)
    eye = target == lane
    sub8 = lax.broadcasted_iota(jnp.int32, (8, 128), 0)
    top_row = jnp.sum(jnp.where(eye, top, 0.0), axis=0, keepdims=True)
    total_row = jnp.sum(jnp.where(eye, total, 0.0), axis=0, keepdims=True)
    stats[0] = jnp.where(sub8 == 0, top_row, total_row)
    copies = [
        remote(stats.at[0], stats.at[PIECE[((-db) % B, (-dy) % Y)]], device(dy=dy, db=db)) for db, dy in ring_p
    ]
    for copy in copies:
        copy.wait_recv()
    best = stats[0, 0:1, :]
    for index in range(1, PIECES):
        best = jnp.maximum(best, stats[index, 0:1, :])
    full = jnp.zeros_like(best)
    for index in range(PIECES):
        full = full + stats[index, 1:2, :] * jnp.exp(stats[index, 0:1, :] - best)
    log_row = best + jnp.log(full)
    log_col = jnp.sum(jnp.where(eye, log_row, 0.0), axis=1, keepdims=True)
    loglik[...] = jnp.broadcast_to(log_col[0:block], (block, 128))
    probs = cot * jnp.exp(scores - log_col)
    rounded = probs.astype(BF16)
    pall[0, 0, 0] = rounded
    back = rounded.astype(F32)
    sums = [
        jnp.sum(jnp.where(ids == float(c), back, 0.0), axis=0, keepdims=True) for c in range(norms.shape[0])
    ]
    sums.append(jnp.broadcast_to(jnp.sum(probs, axis=0, keepdims=True), (8, depth)))

    copies = [
        remote(pall.at[0, 0, 0], pall.at[0, 0, (-dz) % ZZ], device(dz=dz)) for dz in range(1, ZZ)
    ]
    sum_copies = sum_over(cz, zz, ZZ, jnp.concatenate(sums, axis=0), "dz")
    for copy in copies:
        copy.wait_recv()
    copies = [remote(pall.at[0, 0], pall.at[0, (-dx) % X], device(dx=dx)) for dx in range(1, X)]
    sum_copies = sum_over(cx, x, X, total_of(cz, sum_copies), "dx")
    for copy in copies:
        copy.wait_recv()
    copies = [remote(pall.at[0], pall.at[1], device(dc=1))]
    sum_copies = sum_over(cc, core, CORES, total_of(cx, sum_copies), "dc")

    def expand(dc):
        for dx in range(X):
            for dz in range(ZZ):
                part = pall[dc, dx, dz].astype(F32).reshape(PIECES, block, depth)
                zero = jnp.zeros_like(part)
                left = jnp.concatenate([part, zero], axis=1)
                right = jnp.concatenate([zero, part], axis=1)
                p2[:, dz, dc, dx] = jnp.concatenate([left, right], axis=2).astype(BF16)

    expand(0)
    for copy in copies:
        copy.wait_recv()
    expand(1)
    sums = total_of(cc, sum_copies)
    column = sums[8:9, :]
    orients = 128 * orient_rows
    bin_id = lax.broadcasted_iota(jnp.int32, (orients, depth), 0).astype(F32)
    binned = jnp.sum(jnp.where(bin_id == orient_row, column, 0.0), axis=1, keepdims=True)
    eye128 = lax.broadcasted_iota(jnp.int32, (128, 128), 0) == lax.broadcasted_iota(jnp.int32, (128, 128), 1)
    tile = jnp.zeros((8, 128), F32)
    for index in range(orient_rows):
        part = binned[index * 128 : (index + 1) * 128]
        row = jnp.sum(jnp.where(eye128, part, 0.0), axis=0, keepdims=True)
        tile = jnp.where(sub8 == index, row, tile)
    place = y * B + b
    bins[place] = tile
    bin_copies = [remote(bins.at[place], bins.at[place], device(dy=dy, db=db)) for db, dy in ring_p]

    count = PIECES * FGROUP * rows
    direct = tn_dot(p2[...].reshape(count, 2 * depth), w[...].reshape(count, half))
    class_weight = sums[0:8, :]
    for q in range(2):
        correction = tn_dot(class_weight, square[:, q * half : (q + 1) * half], HIGH)
        wide = t2[q].reshape(depth, half).astype(F32)
        value = direct[q * depth : (q + 1) * depth] - wide * correction
        gout[q] = value.astype(BF16).reshape(K, own_t, half)
    copies, local = [], []
    for q in range(2):
        place_q = pl.ds(pl.multiple_of(k * cols + q * half, 128), half)
        local.append(here(gout.at[q, k], grad.at[:, place_q]))
        for da, dc in ring_k:
            dev, k2 = device_k(da, dc)
            copies.append(remote(gout.at[q, k2], grad.at[:, place_q], dev))
    prior[...] = total_of(bins, bin_copies)
    for copy in copies:
        copy.wait_recv()
    for copy in local:
        copy.wait()
    for copy in sent:
        copy.wait_send()


def local(images, ctf_ids, cotangent, templates, template_orient, ctf_table, log_prior):
    classes, width = ctf_table.shape
    orients = log_prior.shape[0]
    own_rows, own_t = images.shape[0], templates.shape[0]
    own_hot = (ctf_ids[:, None] == jnp.arange(classes, dtype=jnp.int32)[None, :]).astype(F32)
    own_ctf = jnp.dot(own_hot, ctf_table, precision=HIGH)
    weighted = (own_ctf * images.astype(F32)).astype(BF16)
    slices = ZH * X * K
    half = width // slices // 2
    rows = 2 * own_rows
    wsrc = weighted.reshape(own_rows, slices, 2, half).transpose(1, 2, 0, 3).reshape(slices, rows, half)
    cot = cotangent.astype(BF16).astype(F32)
    meta = jnp.concatenate(
        [
            jnp.broadcast_to(ctf_ids.astype(F32)[:, None], (own_rows, 64)),
            jnp.broadcast_to(cot[:, None], (own_rows, 64)),
        ],
        axis=1,
    )
    orient_hot = (template_orient[:, None] == jnp.arange(orients, dtype=jnp.int32)[None, :]).astype(F32)
    terms = jnp.dot(orient_hot, log_prior, precision=HIGH)
    tmeta = jnp.stack([terms, template_orient.astype(F32)])
    tmeta = jnp.pad(jnp.concatenate([tmeta, tmeta], axis=1), ((0, 6), (0, 0)))
    depth = K * own_t
    cols = 2 * half
    vmem, anywhere = pl.BlockSpec(memory_space=pltpu.VMEM), pl.BlockSpec(memory_space=pl.ANY)
    grad, loglik, prior = pl.pallas_call(
        kernel,
        out_shape=(
            jax.ShapeDtypeStruct((own_t, K * cols), BF16),
            jax.ShapeDtypeStruct((own_rows, 128), F32),
            jax.ShapeDtypeStruct((8, 128), F32),
        ),
        in_specs=[vmem, anywhere, anywhere, vmem, vmem],
        out_specs=(anywhere, vmem, vmem),
        scratch_shapes=[
            pltpu.VMEM((PIECES, ZZ, CORES, X, rows, half), BF16),
            pltpu.VMEM((CORES, X, ZZ, PIECES, own_rows, depth), F32),
            pltpu.VMEM((X, ZZ, PIECES, own_rows, depth), F32),
            pltpu.VMEM((X - 1, ZZ, PIECES, own_rows, depth), F32),
            pltpu.VMEM((ZZ - 1, PIECES, own_rows, depth), F32),
            pltpu.VMEM((2, K, own_t, half), BF16),
            pltpu.VMEM((classes, cols), F32),
            pltpu.VMEM((PIECES, own_rows, 128), F32),
            pltpu.VMEM((K, 8, 128), F32),
            pltpu.VMEM((ZZ, 8, depth), F32),
            pltpu.VMEM((X, 8, depth), F32),
            pltpu.VMEM((CORES, 8, depth), F32),
            pltpu.VMEM((ZZ, 16, depth), F32),
            pltpu.VMEM((X, 16, depth), F32),
            pltpu.VMEM((CORES, 16, depth), F32),
            pltpu.VMEM((PIECES, 8, 128), F32),
            pltpu.VMEM((PIECES, 8, 128), F32),
            pltpu.VMEM((CORES, X, ZZ, PIECES * own_rows, depth), BF16),
            pltpu.VMEM((PIECES, ZZ, CORES, X, rows, 2 * depth), BF16),
            pltpu.VMEM((2, K, own_t, half), BF16),
            pltpu.SemaphoreType.DMA((400,)),
        ],
        compiler_params=pltpu.CompilerParams(
            collective_id=0, has_side_effects=True, vmem_limit_bytes=50 * 1024 * 1024
        ),
        cost_estimate=pl.CostEstimate(flops=4 * 10**9, bytes_accessed=4 * 10**6, transcendentals=0),
    )(wsrc, templates, ctf_table, meta, tmeta)
    return grad, loglik[:, 0], prior[: orients // 128].reshape(orients)


def solution(mesh):
    placed = (
        P(("tmpl", "img"), None),
        P(("tmpl", "img")),
        P(("tmpl", "img")),
        P("tmpl", None),
        P("tmpl"),
        P(),
        P(),
    )
    return jax.shard_map(
        local,
        mesh=mesh,
        in_specs=placed,
        out_specs=(P("tmpl", "img"), P(("tmpl", "img")), P()),
        check_vma=False,
    )
```

time: 320 us -> 126 us (0.39)
  blocking collectives: 188 us -> 0 us
  Pallas kernels: 0 us -> 116 us
  waiting for transfers between devices: 72.3 us -> 0 us
  matrix products: 42.6 us -> 2.87 us
  between operations: 14.1 us -> 0.67 us
  local copies, waits for them, and re-layouts: 0.71 us -> 4.03 us
    pallas_call x0 -> x1, Pallas kernels: none -> 116 us  [local(): pl.pallas_call(kernel, out_shape=(jax.ShapeDtypeStruct((own_t, K * cols),...]
    psum x1 -> x0, blocking collectives: 98.9 us -> none  [local(): prior_grad = lax.psum(prior_local, ('tmpl', 'img'))]
    all_gather x2 -> x0, blocking collectives: 88.9 us -> none  [the longest x1 46.1 us: local(): small = lax.all_gather(small, 'tmpl', axis=0, tiled=True)]
    all_gather x1 -> x0, waiting for transfers between devices: 47.6 us -> none  [local(): weighted = lax.all_gather(weighted, 'tmpl', axis=0, tiled=True)]
    dot_general x8 -> x1, matrix products: 39.8 us -> 0.84 us  [local(): terms = jnp.dot(orient_hot, log_prior, precision=HIGH)]
    reduce_scatter x1 -> x0, waiting for transfers between devices: 24.7 us -> none  [local(): lax.psum_scatter(partial_value.astype(jnp.bfloat16), 'img', scatter_dimen...]
  transfers between devices with their start and end apart: 2 -> 0, of which waited for: 2 -> 0; matrix products, arithmetic and copies ran while one was open for 4% -> 0% of each run, Pallas kernels for 0% -> 0%
where the time goes in v2:
time: 126 us
  Pallas kernels  116 us (92%)
  local copies, waits for them, and re-layouts  4.03 us (3%)
  matrix products  2.87 us (2%)
  other arithmetic  2.11 us (2%)
    pallas_call x1, Pallas kernels, local(): pl.pallas_call(kernel, out_shape=(jax.ShapeDtypeStruct((own_t, K * cols),...  116 us
    unnamed x5, local copies, waits for them, and re-layouts  2.69 us

profile of v2, /device:TPU:1, one launch (start us, length us, event | category | flops | bytes accessed | tf_op | source)
XLA Modules:
  0.0 126.1 jit_solution(4366397472694649263)
XLA Ops:
  0.6 0.0 copy-start
  0.6 0.7 copy-done
  1.3 0.7 convert_convert_fusion
  2.0 0.8 fusion.1
  2.8 0.7 convert_element_type.24
  3.5 0.7 convert_bitcast_fusion
  4.2 0.1 broadcast_in_dim.4
  4.3 0.1 broadcast_in_dim.5
  4.3 0.1 fusion.3
  4.4 2.0 %fusion = bf16[8,32768]{1,0:T(8,128)(2,1)S(1)} fusion(f32[8,32768]{1,0:T(8,128)} %ctf.1, bf16[8,32768]{1,0:T(8,128)(2,1)} %param.7, s32[8]{0:T(128)} %param.8), kind=kOutput, calls=%fused_computation.1 | convolution fusion | flops 25952320 | bytes 2097184 | tf_op jit(solution)/shard_map/dot_general | solution.py:378
  6.4 0.0 copy-start.1
  6.5 1.2 copy-done.1
  7.7 116.4 %shard_map.94 = (bf16[64,4096]{1,0:T(8,128)(2,1)S(1)}, f32[8,128]{1,0:T(8,128)S(1)}, f32[8,128]{1,0:T(8,128)S(1)}) custom-call(bf16[32,16,512]{2,1,0:T(8,128)(2,1)S(1)} %bitcast.14, bf16[64,32768]{1,0:T(8,128)(2,1)} %templates.1, f32[8,32768]{1,0:T(8,128)S(1)} %copy-done.1, f32[8,128]{1,0:T(8,128)S(1)} %get-tuple-element.10.meta, ...), custom_call_target="tpu_custom_call" | custom-call | flops 4000000000 | bytes 4000000 | tf_op jit(solution)/shard_map/pallas_call | solution.py:399
  124.1 0.6 slice_reduce_fusion
  124.7 0.6 slice_bitcast_fusion
  125.3 0.8 copy.11
Async XLA Ops:
  0.6 0.7 copy-start
  6.4 1.2 copy-start.1

commit v3 on v2

v3 whole, which is shorter than its diff:
```python
import functools

import jax
import jax.numpy as jnp
from jax import lax
from jax.experimental import pallas as pl
from jax.experimental.pallas import tpu as pltpu
from jax.sharding import PartitionSpec as P

HIGH = lax.Precision.HIGHEST
MESH = pl.DeviceIdType.MESH
F32, BF16 = jnp.float32, jnp.bfloat16

Y, ZL, CORES, ZH, X = 4, 4, 2, 2, 4
A = 2
B = ZL // A
ZZ = ZH * A
K = A * CORES
PIECES = Y * B
FGROUP = ZZ * X * CORES

ORDER = (
    [(db, 0) for db in range(B)]
    + [(db, dy) for db in range(B) for dy in (1, 3)]
    + [(db, 2) for db in range(B)]
)
PIECE = {step: index for index, step in enumerate(ORDER)}
Y_FIRST = ()
assert B == 2
GROUPS = (0, 2, 4, 6)


def nt_dot(a, b, precision=None):
    return lax.dot_general(
        a, b, (((1,), (1,)), ((), ())), precision=precision, preferred_element_type=F32
    )


def tn_dot(a, b, precision=None):
    return lax.dot_general(
        a, b, (((0,), (0,)), ((), ())), precision=precision, preferred_element_type=F32
    )


def column_of(row, size):
    wide = jnp.broadcast_to(row, (size, row.shape[1]))
    sub = lax.broadcasted_iota(jnp.int32, wide.shape, 0)
    lane = lax.broadcasted_iota(jnp.int32, wide.shape, 1)
    return jnp.sum(jnp.where(sub == lane, wide, 0.0), axis=1, keepdims=True)


def kernel(
    images, ids_hbm, cot_hbm, templates, orient_hbm, ctf, prior_hbm, grad, loglik, prior,
    own, table, ids_in, cot_in, orient_in, log_prior, cot_round, wsrc, w, s, r1, r2, r3, r4, t2, metas, tmetas, nz, nx, nc, cz, cx, cc, csum, stats, bins,
    pall, p2, gacc, gout, sems,
):
    t, g = lax.axis_index("tmpl"), lax.axis_index("img")
    core, zl, y = t % CORES, (t // CORES) % ZL, t // (CORES * ZL)
    x, zh = g % X, g // X
    a, b = zl // B, zl % B
    zz = zh * A + a
    k = a * CORES + core
    rows, half = w.shape[-2], w.shape[-1]
    block = rows // 2
    cols = 2 * half
    depth, orient_rows = s.shape[-1], 4
    own_t = templates.shape[0]
    owned = PIECES * block

    def device(dy=0, db=0, dz=0, dx=0, dc=0):
        y2, b2, z2, x2, c2 = (y + dy) % Y, (b + db) % B, (zz + dz) % ZZ, (x + dx) % X, (core + dc) % CORES
        zl2 = (z2 % A) * B + b2
        return ((y2 * ZL + zl2) * CORES + c2, (z2 // A) * X + x2)

    def device_k(da, dc):
        a2, c2 = (a + da) % A, (core + dc) % CORES
        return ((y * ZL + a2 * B + b) * CORES + c2, g), a2 * CORES + c2

    used = [0]
    sent = []

    def take():
        used[0] += 1
        return sems.at[used[0] - 1]

    def remote(src, dst, dev):
        copy = pltpu.make_async_remote_copy(
            src_ref=src, dst_ref=dst, send_sem=take(), recv_sem=take(),
            device_id=dev, device_id_type=MESH,
        )
        copy.start()
        sent.append(copy)
        return copy

    def here(src, dst):
        copy = pltpu.make_async_copy(src, dst, take())
        copy.start()
        return copy

    ring_f = [(dz, dx, dc) for dz in range(ZZ) for dx in range(X) for dc in range(CORES)][1:]
    ring_p = ORDER[1:]
    ring_k = [(da, dc) for da in range(A) for dc in range(CORES)][1:]

    load_own = [
        here(ids_hbm, ids_in), here(cot_hbm, cot_in), here(images, own), here(ctf, table),
        here(orient_hbm, orient_in), here(prior_hbm, log_prior),
    ]
    mine = pl.multiple_of((g * K + k) * cols, 128)
    load_t = [
        here(templates.at[:, pl.ds(pl.multiple_of(mine + q * half, 128), half)], t2.at[q, k])
        for q in range(2)
    ]
    barrier = pltpu.get_barrier_semaphore()
    for dz, dx, dc in ring_f:
        pl.semaphore_signal(barrier, inc=1, device_id=device(dz=dz, dx=dx, dc=dc), device_id_type=MESH)
    for db, dy in ring_p:
        pl.semaphore_signal(barrier, inc=1, device_id=device(dy=dy, db=db), device_id_type=MESH)
    for copy in load_own:
        copy.wait()

    ids_own = column_of(ids_in[...].astype(F32), block)
    cot_round[...] = jnp.broadcast_to(column_of(cot_in[...], block), cot_round.shape).astype(BF16)
    cot_own = cot_round[...].astype(F32)[:, 0:1]

    @pl.loop(0, wsrc.shape[0])
    def _(index):
        span = pl.ds(pl.multiple_of(index * cols, 128), cols)
        weight = jnp.broadcast_to(table[0:1, span], (block, cols))
        for c in range(1, table.shape[0]):
            weight = jnp.where(ids_own == float(c), table[c : c + 1, span], weight)
        value = weight * own[:, span].astype(F32)
        wsrc[index] = jnp.concatenate([value[:, :half], value[:, half:]], axis=0).astype(BF16)

    lane8 = lax.broadcasted_iota(jnp.int32, (block, 128), 1)
    metas[0] = jnp.where(lane8 < 64, ids_own, cot_own)
    pl.semaphore_wait(barrier, len(ring_f) + len(ring_p))

    exchange = {}
    z_order = sorted(range(ZZ), key=lambda dz: min(dz, ZZ - dz))
    own_copy = here(wsrc.at[g * K + k], w.at[0, 0, 0, 0])
    for dz in z_order:
        for dx in range(X):
            for dc in range(CORES):
                if (dz, dx, dc) == (0, 0, 0):
                    continue
                z2, x2, c2 = (zz + dz) % ZZ, (x + dx) % X, (core + dc) % CORES
                dest = ((z2 // A) * X + x2) * K + (z2 % A) * CORES + c2
                back = ((-dz) % ZZ, (-dc) % CORES, (-dx) % X)
                exchange.setdefault(back[0], []).append(
                    remote(wsrc.at[dest], w.at[0, back[0], back[1], back[2]], device(dz=dz, dx=dx, dc=dc))
                )

    from_b, from_y = {}, {}

    def send_y(db, dz):
        piece = PIECE[(db, 0)]
        for step in (1, 3):
            from_y[(db, (-step) % Y, dz)] = remote(
                w.at[piece, dz], w.at[PIECE[(db, (-step) % Y)], dz], device(dy=step)
            )

    own_copy.wait()
    for dz in z_order:
        for copy in exchange[dz]:
            copy.wait_recv()
        for db in range(1, B):
            from_b[((-db) % B, dz)] = remote(
                w.at[0, dz], w.at[PIECE[((-db) % B, 0)], dz], device(db=db)
            )
        send_y(0, dz)

    def sum_over(buffer, me, size, value, name):
        buffer[me] = value
        return [
            remote(buffer.at[me], buffer.at[me], device(**{name: step})) for step in range(1, size)
        ]

    def total_of(buffer, copies):
        for copy in copies:
            copy.wait_recv()
        total = buffer[0]
        for index in range(1, buffer.shape[0]):
            total = total + buffer[index]
        return total

    def reduce_core(first):
        span = pl.ds(first, B)
        return remote(s.at[1, :, :, span], r1.at[:, :, span], device(dc=1))

    def reduce_x(first, copy):
        span = pl.ds(first, B)
        copy.wait_recv()
        s[0, :, :, span] = s[0, :, :, span] + r1[:, :, span]
        return [
            remote(s.at[0, dx, :, span], r2.at[dx - 1, :, span], device(dx=dx)) for dx in range(1, X)
        ]

    def reduce_z(first, copies):
        span = pl.ds(first, B)
        for copy in copies:
            copy.wait_recv()
        total = s[0, 0, :, span]
        for index in range(X - 1):
            total = total + r2[index, :, span]
        s[0, 0, :, span] = total
        return [
            remote(s.at[0, 0, dz, span], r3.at[dz - 1, span], device(dz=dz)) for dz in range(1, ZZ)
        ]

    def score(piece):
        lhs = w[piece].reshape(FGROUP * rows, half)
        out = nt_dot(lhs, t2[...].reshape(2 * depth, half))
        out = out.reshape(ZZ, CORES, X, 2, block, 2 * depth)
        value = out[:, :, :, 0, :, :depth] + out[:, :, :, 1, :, depth:]
        for dz in range(ZZ):
            for dc in range(CORES):
                for dx in range(X):
                    s[dc, dx, dz, piece] = value[dz, dc, dx]

    orients = 128 * orient_rows
    orient_own = orient_in[...].astype(F32)
    orient_own = jnp.concatenate([orient_own, orient_own], axis=1)
    bin_id = lax.broadcasted_iota(jnp.int32, (orients, 128), 0).astype(F32)
    level = jnp.concatenate(
        [column_of(log_prior[index : index + 1, :], 128) for index in range(orient_rows)], axis=0
    )
    terms = jnp.sum(jnp.where(bin_id == orient_own, level, 0.0), axis=0, keepdims=True)
    sub8 = lax.broadcasted_iota(jnp.int32, (8, 128), 0)
    tmetas[k] = jnp.where(sub8 == 0, terms, orient_own)
    exchange_t, exchange_tm = [], []
    for da, dc in ring_k:
        dev, k2 = device_k(da, dc)
        for q in range(2):
            start = pl.multiple_of((g * K + k2) * cols + q * half, 128)
            exchange_t.append(remote(templates.at[:, pl.ds(start, half)], t2.at[q, k], dev))
        exchange_tm.append(remote(tmetas.at[k], tmetas.at[k], dev))
    exchange_m = [
        remote(metas.at[0], metas.at[PIECE[((-db) % B, (-dy) % Y)]], device(dy=dy, db=db)) for db, dy in ring_p
    ]

    far = {}

    def send_far(db, dz):
        for side, step in ((0, 1), (1, 3)):
            source = (-step) % Y
            from_y[(db, source, dz)].wait_recv()
            far[(db, dz, side)] = remote(
                w.at[PIECE[(db, source)], dz, side], w.at[PIECE[(db, 2)], dz, side], device(dy=step)
            )

    across = {}
    for dz in z_order:
        from_b[(1, dz)].wait_recv()
        if dz not in Y_FIRST:
            send_y(1, dz)
        send_far(0, dz)
        if dz in Y_FIRST:
            for dy in (1, 3):
                across[(dy, dz)] = remote(
                    w.at[PIECE[(0, dy)], dz], w.at[PIECE[(1, dy)], dz], device(db=1)
                )

    for copy in load_t:
        copy.wait()
    for copy in exchange_t + exchange_tm + exchange_m:
        copy.wait_recv()
    square = table[:, pl.ds(mine, cols)]
    square = square * square
    norm_part = jnp.zeros((square.shape[0], depth), F32)
    for q in range(2):
        wide = t2[q].reshape(depth, half).astype(F32)
        norm_part += nt_dot(square[:, q * half : (q + 1) * half], wide * wide, HIGH)
    norm_copies = sum_over(nz, zz, ZZ, norm_part, "dz")

    stage = [None] * len(GROUPS)
    for db in range(B):
        score(PIECE[(db, 0)])
    stage[0] = reduce_core(GROUPS[0])
    for dy in (1, 3):
        score(PIECE[(0, dy)])
    stage[0] = reduce_x(GROUPS[0], stage[0])
    stage[1] = reduce_core(GROUPS[1])
    norm_copies = sum_over(nx, x, X, total_of(nz, norm_copies), "dx")
    for dz in z_order:
        if dz not in Y_FIRST:
            send_far(1, dz)
    for dz in Y_FIRST:
        for side in range(2):
            far[(0, dz, side)].wait_recv()
        across[(2, dz)] = remote(w.at[PIECE[(0, 2)], dz], w.at[PIECE[(1, 2)], dz], device(db=1))
    stage[0] = reduce_z(GROUPS[0], stage[0])
    stage[1] = reduce_x(GROUPS[1], stage[1])
    norm_copies = sum_over(nc, core, CORES, total_of(nx, norm_copies), "dc")
    for dy in (1, 3):
        for dz in Y_FIRST:
            across[(dy, dz)].wait_recv()
        score(PIECE[(1, dy)])
    stage[2] = reduce_core(GROUPS[2])
    stage[1] = reduce_z(GROUPS[1], stage[1])
    stage[2] = reduce_x(GROUPS[2], stage[2])
    norms = total_of(nc, norm_copies)
    for db in range(B):
        for dz in z_order:
            if dz not in Y_FIRST:
                for side in range(2):
                    far[(db, dz, side)].wait_recv()
            elif db == 1:
                across[(2, dz)].wait_recv()
        score(PIECE[(db, 2)])
    stage[3] = reduce_core(GROUPS[3])
    stage[2] = reduce_z(GROUPS[2], stage[2])
    stage[3].wait_recv()
    span = pl.ds(GROUPS[3], B)
    s[0, :, :, span] = s[0, :, :, span] + r1[:, :, span]
    stage[3] = [
        remote(s.at[0, dx, dz, span], r4.at[dx * ZZ + dz - 1], device(dx=dx, dz=dz))
        for dz in range(ZZ) for dx in range(X) if (dx, dz) != (0, 0)
    ]
    for copies in stage:
        for copy in copies:
            copy.wait_recv()
    total = s[0, 0, 0, span]
    for index in range(X * ZZ - 1):
        total = total + r4[index]
    s[0, 0, 0, span] = total
    early = PIECES - B
    value = s[0, 0, 0, :early]
    for index in range(ZZ - 1):
        value = value + r3[index]
    s[0, 0, 0, :early] = value
    scores = s[0, 0, 0]
    scores = scores.reshape(owned, depth)

    info = metas[...].reshape(owned, 128)
    ids, cot = info[:, 0:1], info[:, 64:65]
    lane1 = lax.broadcasted_iota(jnp.int32, (1, 128), 1)
    prior_row = jnp.concatenate(
        [jnp.where(lane1 < 64, tmetas[i, 0:1, :], tmetas[i + 1, 0:1, :]) for i in range(0, K, 2)], axis=1
    )
    orient_row = jnp.concatenate(
        [jnp.where(lane1 < 64, tmetas[i, 1:2, :], tmetas[i + 1, 1:2, :]) for i in range(0, K, 2)], axis=1
    )
    norm_rows = jnp.zeros((owned, depth), F32)
    for c in range(norms.shape[0]):
        norm_rows = jnp.where(ids == float(c), norms[c : c + 1, :], norm_rows)
    scores = scores - 0.5 * norm_rows + prior_row
    top = jnp.max(scores, axis=1, keepdims=True)
    total = jnp.sum(jnp.exp(scores - top), axis=1, keepdims=True)
    sub = lax.broadcasted_iota(jnp.int32, (owned, 128), 0)
    lane = lax.broadcasted_iota(jnp.int32, (owned, 128), 1)
    target = sub % block
    for index, (db, dy) in enumerate(ORDER):
        place = ((y + dy) % Y) * B + (b + db) % B
        target = target + jnp.where(sub // block == index, place * block, 0)
    eye = target == lane
    top_row = jnp.sum(jnp.where(eye, top, 0.0), axis=0, keepdims=True)
    total_row = jnp.sum(jnp.where(eye, total, 0.0), axis=0, keepdims=True)
    stats[0] = jnp.where(sub8 == 0, top_row, total_row)
    copies = [
        remote(stats.at[0], stats.at[PIECE[((-db) % B, (-dy) % Y)]], device(dy=dy, db=db)) for db, dy in ring_p
    ]
    for copy in copies:
        copy.wait_recv()
    best = stats[0, 0:1, :]
    for index in range(1, PIECES):
        best = jnp.maximum(best, stats[index, 0:1, :])
    full = jnp.zeros_like(best)
    for index in range(PIECES):
        full = full + stats[index, 1:2, :] * jnp.exp(stats[index, 0:1, :] - best)
    log_row = best + jnp.log(full)
    log_col = jnp.sum(jnp.where(eye, log_row, 0.0), axis=1, keepdims=True)
    loglik[...] = jnp.broadcast_to(log_col[0:block], (block, 128))
    probs = cot * jnp.exp(scores - log_col)
    rounded = probs.astype(BF16)
    pall[0, 0, 0] = rounded

    def send_x(dz):
        return [
            remote(pall.at[0, 0, dz], pall.at[0, (-dx) % X, dz], device(dx=dx)) for dx in range(1, X)
        ]

    on_z = {
        (-dz) % ZZ: remote(pall.at[0, 0, 0], pall.at[0, 0, (-dz) % ZZ], device(dz=dz)) for dz in range(1, ZZ)
    }
    on_x = {0: send_x(0)}
    sums = [
        jnp.sum(jnp.where(ids == float(c), probs, 0.0), axis=0, keepdims=True) for c in range(norms.shape[0])
    ]
    sum_copies = sum_over(cz, zz, ZZ, jnp.concatenate(sums, axis=0), "dz")

    far_a = (a + 1) % A
    lanes = CORES * own_t

    def expand(dc, dz, side, which):
        span = pl.ds(pl.multiple_of(which * lanes, 128), lanes)
        for dx in range(X):
            part = pall[dc, dx, dz, :, span].astype(F32).reshape(PIECES, block, lanes)
            zero = jnp.zeros_like(part)
            left = jnp.concatenate([part, zero], axis=1)
            right = jnp.concatenate([zero, part], axis=1)
            p2[side, :, dx] = jnp.concatenate([left, right], axis=2).astype(BF16)

    def add_block(dc, dz, side, first=False):
        which = far_a if side == 0 else a
        expand(dc, dz, side, which)
        count = PIECES * X * rows
        value = tn_dot(p2[side].reshape(count, 2 * lanes), w[:, dz, dc].reshape(count, half))
        gacc[side] = value if first else gacc[side] + value

    for dz in z_order[1:]:
        on_z[dz].wait_recv()
        on_x[dz] = send_x(dz)
    sum_copies = sum_over(cx, x, X, total_of(cz, sum_copies), "dx")
    on_core = {}
    for dz in z_order:
        for copy in on_x[dz]:
            copy.wait_recv()
        on_core[dz] = remote(pall.at[0, :, dz], pall.at[1, :, dz], device(dc=1))
        if dz == z_order[0]:
            sum_copies = sum_over(cc, core, CORES, total_of(cx, sum_copies), "dc")
    for dz in z_order:
        add_block(0, dz, 0, dz == z_order[0])
    sums = total_of(cc, sum_copies)
    column = jnp.sum(sums, axis=0, keepdims=True)
    bin_id = lax.broadcasted_iota(jnp.int32, (orients, depth), 0).astype(F32)
    binned = jnp.sum(jnp.where(bin_id == orient_row, column, 0.0), axis=1, keepdims=True)
    eye128 = lax.broadcasted_iota(jnp.int32, (128, 128), 0) == lax.broadcasted_iota(jnp.int32, (128, 128), 1)
    tile = jnp.zeros((8, 128), F32)
    for index in range(orient_rows):
        part = binned[index * 128 : (index + 1) * 128]
        row = jnp.sum(jnp.where(eye128, part, 0.0), axis=0, keepdims=True)
        tile = jnp.where(sub8 == index, row, tile)
    place = y * B + b
    bins[place] = tile
    bin_copies = [remote(bins.at[place], bins.at[place], device(dy=dy, db=db)) for db, dy in ring_p]

    csum[...] = sums
    for dz in z_order:
        on_core[dz].wait_recv()
        add_block(1, dz, 0)
    copies, local = [], []
    for side in range(2):
        if side == 1:
            for dc in range(CORES):
                for dz in z_order:
                    add_block(dc, dz, 1, (dc, dz) == (0, z_order[0]))
        which = far_a if side == 0 else a
        span = pl.ds(pl.multiple_of(which * lanes, 128), lanes)
        class_weight = csum[:, span]
        for q in range(2):
            correction = tn_dot(class_weight, square[:, q * half : (q + 1) * half], HIGH)
            wide = t2[q, pl.ds(which * CORES, CORES)].reshape(lanes, half).astype(F32)
            value = gacc[side, q * lanes : (q + 1) * lanes] - wide * correction
            gout[side, q] = value.astype(BF16).reshape(CORES, own_t, half)
        for q in range(2):
            place_q = pl.ds(pl.multiple_of(k * cols + q * half, 128), half)
            for dc in range(CORES):
                dest = (core + dc) % CORES
                if (side, dc) == (1, 0):
                    local.append(here(gout.at[side, q, dest], grad.at[:, place_q]))
                else:
                    dev, _ = device_k(1 - side, dc)
                    copies.append(remote(gout.at[side, q, dest], grad.at[:, place_q], dev))
    prior[...] = total_of(bins, bin_copies)
    for copy in copies:
        copy.wait_recv()
    for copy in local:
        copy.wait()
    for copy in sent:
        copy.wait_send()


def local(images, ctf_ids, cotangent, templates, template_orient, ctf_table, log_prior):
    classes, width = ctf_table.shape
    orients = log_prior.shape[0]
    own_rows, own_t = images.shape[0], templates.shape[0]
    slices = ZH * X * K
    half = width // slices // 2
    rows = 2 * own_rows
    lanes = CORES * own_t
    depth = K * own_t
    cols = 2 * half
    vmem, anywhere = pl.BlockSpec(memory_space=pltpu.VMEM), pl.BlockSpec(memory_space=pl.ANY)
    grad, loglik, prior = pl.pallas_call(
        kernel,
        out_shape=(
            jax.ShapeDtypeStruct((own_t, K * cols), BF16),
            jax.ShapeDtypeStruct((own_rows, 128), F32),
            jax.ShapeDtypeStruct((8, 128), F32),
        ),
        in_specs=[pl.BlockSpec(memory_space=pltpu.HBM)] * 7,
        out_specs=(anywhere, vmem, vmem),
        scratch_shapes=[
            pltpu.VMEM((own_rows, width), BF16),
            pltpu.VMEM((classes, width), F32),
            pltpu.VMEM((1, own_rows), jnp.int32),
            pltpu.VMEM((1, own_rows), F32),
            pltpu.VMEM((1, own_t), jnp.int32),
            pltpu.VMEM((orients // 128, 128), F32),
            pltpu.VMEM((own_rows, 128), BF16),
            pltpu.VMEM((slices, rows, half), BF16),
            pltpu.VMEM((PIECES, ZZ, CORES, X, rows, half), BF16),
            pltpu.VMEM((CORES, X, ZZ, PIECES, own_rows, depth), F32),
            pltpu.VMEM((X, ZZ, PIECES, own_rows, depth), F32),
            pltpu.VMEM((X - 1, ZZ, PIECES - B, own_rows, depth), F32),
            pltpu.VMEM((ZZ - 1, PIECES - B, own_rows, depth), F32),
            pltpu.VMEM((X * ZZ - 1, B, own_rows, depth), F32),
            pltpu.VMEM((2, K, own_t, half), BF16),
            pltpu.VMEM((PIECES, own_rows, 128), F32),
            pltpu.VMEM((K, 8, 128), F32),
            pltpu.VMEM((ZZ, 8, depth), F32),
            pltpu.VMEM((X, 8, depth), F32),
            pltpu.VMEM((CORES, 8, depth), F32),
            pltpu.VMEM((ZZ, 8, depth), F32),
            pltpu.VMEM((X, 8, depth), F32),
            pltpu.VMEM((CORES, 8, depth), F32),
            pltpu.VMEM((8, depth), F32),
            pltpu.VMEM((PIECES, 8, 128), F32),
            pltpu.VMEM((PIECES, 8, 128), F32),
            pltpu.VMEM((CORES, X, ZZ, PIECES * own_rows, depth), BF16),
            pltpu.VMEM((2, PIECES, X, rows, 2 * lanes), BF16),
            pltpu.VMEM((2, 2 * lanes, half), F32),
            pltpu.VMEM((2, 2, CORES, own_t, half), BF16),
            pltpu.SemaphoreType.DMA((400,)),
        ],
        compiler_params=pltpu.CompilerParams(
            collective_id=0, has_side_effects=True, vmem_limit_bytes=56 * 1024 * 1024
        ),
        cost_estimate=pl.CostEstimate(flops=4 * 10**9, bytes_accessed=4 * 10**6, transcendentals=0),
    )(
        images,
        ctf_ids.reshape(1, own_rows),
        cotangent.reshape(1, own_rows),
        templates,
        template_orient.reshape(1, own_t),
        ctf_table,
        log_prior.reshape(orients // 128, 128),
    )
    return grad, loglik[:, 0], prior[: orients // 128].reshape(orients)


def solution(mesh):
    placed = (
        P(("tmpl", "img"), None),
        P(("tmpl", "img")),
        P(("tmpl", "img")),
        P("tmpl", None),
        P("tmpl"),
        P(),
        P(),
    )
    return jax.shard_map(
        local,
        mesh=mesh,
        in_specs=placed,
        out_specs=(P("tmpl", "img"), P(("tmpl", "img")), P()),
        check_vma=False,
    )
```

time: 126 us -> 113 us (0.90)
  Pallas kernels: 116 us -> 108 us
  matrix products: 2.87 us -> 0 us
  other arithmetic: 2.11 us -> 0 us
    pallas_call x1, Pallas kernels: 116 us -> 108 us  [local(): pl.pallas_call(kernel, out_shape=(jax.ShapeDtypeStruct((own_t, K * cols),...]
    dot_general x2 -> x0, matrix products: 2.87 us -> none  [the longest x1 2.03 us: local(): own_ctf = jnp.dot(own_hot, ctf_table, precision=HIGH)]
    convert_element_type x2 -> x0, other arithmetic: 1.37 us -> none  [the longest x1 0.72 us: local(): ctf_ids.astype(F32)[:, None]]
    unnamed x5 -> x1, local copies, waits for them, and re-layouts: 2.69 us -> 1.87 us
where the time goes in v3:
time: 113 us
  Pallas kernels  108 us (96%)
  local copies, waits for them, and re-layouts  4.43 us (4%)
    pallas_call x1, Pallas kernels, local(): pl.pallas_call(kernel, out_shape=(jax.ShapeDtypeStruct((own_t, K * cols),...  108 us

profile of v3, /device:TPU:1, one launch (start us, length us, event | category | flops | bytes accessed | tf_op | source)
XLA Modules:
  0.0 113.1 jit_solution(11507127966371132461)
XLA Ops:
  0.6 108.0 %shard_map.94 = (bf16[64,4096]{1,0:T(8,128)(2,1)}, f32[8,128]{1,0:T(8,128)}, f32[8,128]{1,0:T(8,128)}) custom-call(bf16[8,32768]{1,0:T(8,128)(2,1)} %images.1, s32[1,8]{1,0:T(1,128)} %bitcast.7, f32[1,8]{1,0:T(1,128)} %bitcast.8, bf16[64,32768]{1,0:T(8,128)(2,1)} %templates.1, s32[1,64]{1,0:T(1,128)} %bitcast.9, f32[8,32768]{1,0:T(8,128)} %ctf.1, ...), custom_call_target="tpu_custom_call" | custom-call | flops 4000000000 | bytes 4000000 | tf_op jit(solution)/shard_map/pallas_call | solution.py:484
  108.6 1.3 %slice_reduce_fusion = f32[8]{0:T(128)} fusion(f32[8,128]{1,0:T(8,128)} %get-tuple-element.7), kind=kLoop, calls=%fused_computation | loop fusion | bytes 64 | tf_op jit(solution)/shard_map/slice | solution.py:539
  110.0 1.3 %slice_bitcast_fusion = f32[512]{0:T(512)} fusion(f32[8,128]{1,0:T(8,128)} %get-tuple-element.8), kind=kLoop, calls=%fused_computation.1 | loop fusion | bytes 4096 | tf_op jit(solution)/shard_map/reshape | solution.py:539
  111.2 1.9 %copy.11 = bf16[64,4096]{1,0:T(8,128)(2,1)} copy(bf16[64,4096]{1,0:T(8,128)(2,1)} %get-tuple-element.12) | data formatting | bytes 1048576

commit v4 on v3

--- a/solution.py
+++ b/solution.py
@@ -288,15 +288,14 @@
         for side in range(2):
             far[(0, dz, side)].wait_recv()
         across[(2, dz)] = remote(w.at[PIECE[(0, 2)], dz], w.at[PIECE[(1, 2)], dz], device(db=1))
+    stage[1] = reduce_x(GROUPS[1], stage[1])
     stage[0] = reduce_z(GROUPS[0], stage[0])
-    stage[1] = reduce_x(GROUPS[1], stage[1])
     norm_copies = sum_over(nc, core, CORES, total_of(nx, norm_copies), "dc")
     for dy in (1, 3):
         for dz in Y_FIRST:
             across[(dy, dz)].wait_recv()
         score(PIECE[(1, dy)])
     stage[2] = reduce_core(GROUPS[2])
-    stage[1] = reduce_z(GROUPS[1], stage[1])
     stage[2] = reduce_x(GROUPS[2], stage[2])
     norms = total_of(nc, norm_copies)
     for db in range(B):
@@ -308,7 +307,6 @@
                 across[(2, dz)].wait_recv()
         score(PIECE[(db, 2)])
     stage[3] = reduce_core(GROUPS[3])
-    stage[2] = reduce_z(GROUPS[2], stage[2])
     stage[3].wait_recv()
     span = pl.ds(GROUPS[3], B)
     s[0, :, :, span] = s[0, :, :, span] + r1[:, :, span]
@@ -316,6 +314,8 @@
         remote(s.at[0, dx, dz, span], r4.at[dx * ZZ + dz - 1], device(dx=dx, dz=dz))
         for dz in range(ZZ) for dx in range(X) if (dx, dz) != (0, 0)
     ]
+    stage[1] = reduce_z(GROUPS[1], stage[1])
+    stage[2] = reduce_z(GROUPS[2], stage[2])
     for copies in stage:
         for copy in copies:
             copy.wait_recv()

time: 113 us -> 111 us (0.982)
  Pallas kernels: 108 us -> 106 us
    pallas_call x1, Pallas kernels: 108 us -> 106 us  [local(): pl.pallas_call(kernel, out_shape=(jax.ShapeDtypeStruct((own_t, K * cols),...]
where the time goes in v4:
time: 111 us
  Pallas kernels  106 us (95%)
  local copies, waits for them, and re-layouts  4.43 us (4%)
    pallas_call x1, Pallas kernels, local(): pl.pallas_call(kernel, out_shape=(jax.ShapeDtypeStruct((own_t, K * cols),...  106 us

profile of v4, /device:TPU:1, one launch (start us, length us, event | category | flops | bytes accessed | tf_op | source)
XLA Modules:
  0.0 111.2 jit_solution(16502030024298056824)
XLA Ops:
  0.6 106.1 %shard_map.94 = (bf16[64,4096]{1,0:T(8,128)(2,1)}, f32[8,128]{1,0:T(8,128)}, f32[8,128]{1,0:T(8,128)}) custom-call(bf16[8,32768]{1,0:T(8,128)(2,1)} %images.1, s32[1,8]{1,0:T(1,128)} %bitcast.7, f32[1,8]{1,0:T(1,128)} %bitcast.8, bf16[64,32768]{1,0:T(8,128)(2,1)} %templates.1, s32[1,64]{1,0:T(1,128)} %bitcast.9, f32[8,32768]{1,0:T(8,128)} %ctf.1, ...), custom_call_target="tpu_custom_call" | custom-call | flops 4000000000 | bytes 4000000 | tf_op jit(solution)/shard_map/pallas_call | solution.py:484
  106.8 1.3 %slice_reduce_fusion = f32[8]{0:T(128)} fusion(f32[8,128]{1,0:T(8,128)} %get-tuple-element.7), kind=kLoop, calls=%fused_computation | loop fusion | bytes 64 | tf_op jit(solution)/shard_map/slice | solution.py:539
  108.1 1.3 %slice_bitcast_fusion = f32[512]{0:T(512)} fusion(f32[8,128]{1,0:T(8,128)} %get-tuple-element.8), kind=kLoop, calls=%fused_computation.1 | loop fusion | bytes 4096 | tf_op jit(solution)/shard_map/reshape | solution.py:539
  109.3 1.9 %copy.11 = bf16[64,4096]{1,0:T(8,128)(2,1)} copy(bf16[64,4096]{1,0:T(8,128)(2,1)} %get-tuple-element.12) | data formatting | bytes 1048576

commit v5 on v4

--- a/solution.py
+++ b/solution.py
@@ -250,10 +250,10 @@
 
     across = {}
     for dz in z_order:
+        send_far(0, dz)
         from_b[(1, dz)].wait_recv()
         if dz not in Y_FIRST:
             send_y(1, dz)
-        send_far(0, dz)
         if dz in Y_FIRST:
             for dy in (1, 3):
                 across[(dy, dz)] = remote(
@@ -461,12 +461,14 @@
                 else:
                     dev, _ = device_k(1 - side, dc)
                     copies.append(remote(gout.at[side, q, dest], grad.at[:, place_q], dev))
+    for copy in sent[: -len(copies)]:
+        copy.wait_send()
     prior[...] = total_of(bins, bin_copies)
     for copy in copies:
         copy.wait_recv()
     for copy in local:
         copy.wait()
-    for copy in sent:
+    for copy in copies:
         copy.wait_send()
 
 

time: 111 us -> 111 us (level)
  no operation moved by 1% of the time
where the time goes in v5:
time: 111 us; the launch traced here: 110 us
  Pallas kernels  105 us (95%)
  local copies, waits for them, and re-layouts  4.43 us (4%)
    pallas_call x1, Pallas kernels, local(): pl.pallas_call(kernel, out_shape=(jax.ShapeDtypeStruct((own_t, K * cols),...  105 us

profile of v5, /device:TPU:1, one launch (start us, length us, event | category | flops | bytes accessed | tf_op | source)
XLA Modules:
  0.0 110.3 jit_solution(4646382189279578504)
XLA Ops:
  0.6 105.3 %shard_map.94 = (bf16[64,4096]{1,0:T(8,128)(2,1)}, f32[8,128]{1,0:T(8,128)}, f32[8,128]{1,0:T(8,128)}) custom-call(bf16[8,32768]{1,0:T(8,128)(2,1)} %images.1, s32[1,8]{1,0:T(1,128)} %bitcast.7, f32[1,8]{1,0:T(1,128)} %bitcast.8, bf16[64,32768]{1,0:T(8,128)(2,1)} %templates.1, s32[1,64]{1,0:T(1,128)} %bitcast.9, f32[8,32768]{1,0:T(8,128)} %ctf.1, ...), custom_call_target="tpu_custom_call" | custom-call | flops 4000000000 | bytes 4000000 | tf_op jit(solution)/shard_map/pallas_call | solution.py:486
  105.9 1.3 %slice_reduce_fusion = f32[8]{0:T(128)} fusion(f32[8,128]{1,0:T(8,128)} %get-tuple-element.7), kind=kLoop, calls=%fused_computation | loop fusion | bytes 64 | tf_op jit(solution)/shard_map/slice | solution.py:541
  107.2 1.3 %slice_bitcast_fusion = f32[512]{0:T(512)} fusion(f32[8,128]{1,0:T(8,128)} %get-tuple-element.8), kind=kLoop, calls=%fused_computation.1 | loop fusion | bytes 4096 | tf_op jit(solution)/shard_map/reshape | solution.py:541
  108.5 1.9 %copy.11 = bf16[64,4096]{1,0:T(8,128)(2,1)} copy(bf16[64,4096]{1,0:T(8,128)(2,1)} %get-tuple-element.12) | data formatting | bytes 1048576
